TPU v7x, 32 devices: a whole 2x2x4 slice. The times are simulated.
32 devices in a mesh: lat: 8 (over z, x), lon: 4 (over y, core).
Axes of the slice: x: 2, y: 2, z: 4, core: 2. Of those that a mesh axis runs over, the one named last changes fastest.
Arguments:
- state: float32 [4, 2, 192, 512], P(None, None, 'lat', 'lon'), may hold values from -6 to 6
- zonal_shift: int32 [2, 192], P(None, 'lat'), may hold values from -256 to 256, as said below
- zonal_cells: int32 [2, 192, 512], P(None, 'lat', 'lon'), may hold values from -2 to 2
- zonal_fraction: float32 [2, 192, 512], P(None, 'lat', 'lon'), may hold values from 0 to 1
- merid_cells: int32 [2, 192, 512], P(None, 'lat', 'lon'), may hold values from -1 to 1
- merid_fraction: float32 [2, 192, 512], P(None, 'lat', 'lon'), may hold values from 0 to 1
- coupling: float32 [2, 192, 512], P(None, 'lat', 'lon'), may hold values from 0.5 to 8
Outputs:
- advanced: float32 [4, 2, 192, 512], P(None, None, 'lat', 'lon')
Inputs may be any that keep to these rules, and one draw needn't show every extreme that they name: `zonal_shift`: one whole-cell zonal displacement for each level and latitude row; bounded more tightly near the equator than near the poles.
All inputs are finite; a program needn't handle non-finite values.
Results may differ from a plain program's by a relative error of at most 0.00002.
Values sent between devices are 32-bit elements; how exact they have to be, the bound alone decides.
A program may use at most 128 MiB of HBM per device.

v0:
```python
import functools

import jax
import jax.numpy as jnp
from jax import lax
from jax.experimental import pallas as pl
from jax.experimental.pallas import tpu as pltpu
from jax.sharding import PartitionSpec as P

SWEEPS = 4
HALO = 8
MESH = pl.DeviceIdType.MESH


def cubic_weights(frac):
    return (
        -frac * (frac - 1.0) * (frac - 2.0) / 6.0,
        (frac + 1.0) * (frac - 1.0) * (frac - 2.0) / 2.0,
        -(frac + 1.0) * frac * (frac - 2.0) / 2.0,
        (frac + 1.0) * frac * (frac - 1.0) / 6.0,
    )


def take_lanes(value, index):
    return jnp.take_along_axis(value, index, axis=1, mode="promise_in_bounds")


def merid_parts(cells, frac):
    w = cubic_weights(frac)
    parts = []
    for offset in range(-2, 4):
        total = jnp.zeros_like(frac)
        for k in range(4):
            cell = k - 1 - offset
            if -1 <= cell <= 1:
                total = jnp.where(cells == float(cell), w[k], total)
        parts.append(total)
    return parts


def kernel(
    bands, sectors, state, shift_in, zcells_in, zfrac_in, mcells_in, mfrac, coup, out,
    ring, zmain, zwest, zeast, pmain, pwest, peast, shift, zcells, zfrac, mcells, loaded,
    y_send, y_recv, p_send, p_recv, h_send, h_recv, z_send, z_recv,
):
    fields, levels, rows, width = state.shape
    both = fields * levels
    halves = sectors // 2
    circle = sectors * width
    la, lo = lax.axis_index("lat"), lax.axis_index("lon")
    half = lo // 2
    core = lo - 2 * half
    partner = lo + 1 - 2 * core
    east = lax.rem(lo + 1, sectors)
    west = lax.rem(lo + sectors - 1, sectors)
    has_north, has_south = la > 0, la < bands - 1
    own = pl.ds(HALO, rows)

    barrier = pltpu.get_barrier_semaphore()

    def greet(to_la, to_lo):
        pl.semaphore_signal(barrier, inc=1, device_id=(to_la, to_lo), device_id_type=MESH)

    greet(la, east)
    greet(la, west)
    others = [2 * lax.rem(half + d, halves) + core for d in range(1, halves)]
    sources = [2 * lax.rem(half + halves - d, halves) + core for d in range(1, halves)]
    for other in others:
        greet(la, other)

    @pl.when(has_north)
    def _():
        for to_lo in (lo, east, west):
            greet(la - 1, to_lo)

    @pl.when(has_south)
    def _():
        for to_lo in (lo, east, west):
            greet(la + 1, to_lo)

    loads = [
        pltpu.make_async_copy(src, dst, loaded.at[i])
        for i, (src, dst) in enumerate((
            (state, ring.at[lo]),
            (mcells_in, mcells),
            (mfrac, pmain.at[pl.ds(levels, levels), own]),
            (coup, pmain.at[pl.ds(2 * levels, levels), own]),
            (shift_in, shift),
            (zcells_in, zcells),
            (zfrac_in, zfrac),
        ))
    ]
    for load in loads:
        load.start()

    for condition, begin in ((la == 0, 0), (la == bands - 1, rows + HALO)):
        @pl.when(condition)
        def _(begin=begin):
            for ref in (zmain, zwest, zeast):
                ref[:, pl.ds(begin, HALO), :] = jnp.zeros((ref.shape[0], HALO, width), jnp.float32)

    loads[0].wait()
    outer = jnp.logical_or(la == 0, la == bands - 1)

    @pl.when(outer)
    def _():
        pl.semaphore_wait(barrier, 1 + halves + 3)

    @pl.when(jnp.logical_not(outer))
    def _():
        pl.semaphore_wait(barrier, 1 + halves + 6)

    def remote(src, dst, send, recv, to_la, to_lo):
        return pltpu.make_async_remote_copy(
            src_ref=src, dst_ref=dst, send_sem=send, recv_sem=recv,
            device_id=(to_la, to_lo), device_id_type=MESH,
        )

    across, beside, relay = {}, {}, {}
    for f in range(fields):
        for d, other in enumerate(others):
            across[f, d] = remote(
                ring.at[lo, f], ring.at[lo, f], y_send.at[d, f], y_recv.at[d, f], la, other
            )
            across[f, d].start()
    for f in range(fields):
        beside[f] = remote(
            ring.at[lo, f], ring.at[lo, f], p_send.at[halves - 1, f], p_recv.at[halves - 1, f], la, partner
        )
        beside[f].start()

    def neighbours(main, to_west, to_east, first, count, send, recv):
        top, bottom = pl.ds(HALO, HALO), pl.ds(rows, HALO)
        before, after = pl.ds(0, HALO), pl.ds(rows + HALO, HALO)
        strip = pl.ds(first, count)
        none = None
        plan = [
            (main.at[strip, top], main.at[strip, after], la - 1, lo, has_north, has_south),
            (main.at[strip, bottom], main.at[strip, before], la + 1, lo, has_south, has_north),
            (main.at[strip, own], to_west.at[:, own], la, east, none, none),
            (main.at[strip, own], to_east.at[:, own], la, west, none, none),
            (main.at[strip, top], to_west.at[:, after], la - 1, east, has_north, has_south),
            (main.at[strip, top], to_east.at[:, after], la - 1, west, has_north, has_south),
            (main.at[strip, bottom], to_west.at[:, before], la + 1, east, has_south, has_north),
            (main.at[strip, bottom], to_east.at[:, before], la + 1, west, has_south, has_north),
        ]
        return [
            (remote(src, dst, send.at[i], recv.at[i], to_la, to_lo), goes, comes)
            for i, (src, dst, to_la, to_lo, goes, comes) in enumerate(plan)
        ]

    def straight(main, part, send, recv):
        top, bottom = pl.ds(HALO, HALO), pl.ds(rows, HALO)
        before, after = pl.ds(0, HALO), pl.ds(rows + HALO, HALO)
        return [
            (remote(main.at[part, top], main.at[part, after], send.at[0], recv.at[0], la - 1, lo),
             has_north, has_south),
            (remote(main.at[part, bottom], main.at[part, before], send.at[1], recv.at[1], la + 1, lo),
             has_south, has_north),
        ]

    def guarded(condition, action):
        if condition is None:
            action()
        else:
            pl.when(condition)(action)

    lane = lax.broadcasted_iota(jnp.int32, (rows, width), 1)
    group = lane // (2 * HALO)
    edge = ((lane & (HALO - 1)) + width - HALO // 2) & (width - 1)
    for load in loads[1:4]:
        load.wait()
    for l in range(levels):
        pmain[l, own] = mcells[l].astype(jnp.float32)
    for at in range(3):
        low, high = pmain[2 * at, own], pmain[2 * at + 1, own]
        packed = jnp.where((group & 1) == 0, take_lanes(low, edge), take_lanes(high, edge))
        pmain[6 + at, own] = packed

    params = straight(pmain, pl.ds(0, 6), h_send.at[pl.ds(8, 2)], h_recv.at[pl.ds(8, 2)])
    params += neighbours(pmain, pwest, peast, 6, 3, h_send, h_recv)
    for copy, goes, _ in params:
        guarded(goes, copy.start)

    for load in loads[4:]:
        load.wait()
    square = (rows, rows)
    diagonal = lax.broadcasted_iota(jnp.int32, square, 0) == lax.broadcasted_iota(jnp.int32, square, 1)
    plans = []
    for l in range(levels):
        line = jnp.broadcast_to(shift[pl.ds(l, 1), :].astype(jnp.float32), square)
        moved = jnp.sum(jnp.where(diagonal, line, 0.0), axis=1, keepdims=True).astype(jnp.int32)
        base = lo * width - 3 - jnp.broadcast_to(moved, (rows, width))
        base = jnp.where(base < 0, base + circle, base)
        base = jnp.where(base >= circle, base - circle, base)
        hop = lax.shift_right_logical(base, width.bit_length() - 1)
        within = base & (width - 1)
        near = hop + jnp.where(lane < within, 1, 0)
        near = jnp.where(near >= sectors, near - sectors, near)
        far = near + 1
        far = jnp.where(far >= sectors, far - sectors, far)
        weights = cubic_weights(zfrac[l])
        cells = zcells[l]
        steps = []
        for k in range(4):
            place = lane + (k + 2) - cells
            steps.append((place >= width, (place + within) & (width - 1), weights[k]))
        plans.append((near, far, steps))

    def zonal_field(f):
        for l in range(levels):
            near, far, steps = plans[l]
            first = second = ring[0, f, l]
            for s in range(1, sectors):
                block = ring[s, f, l]
                first = jnp.where(near == s, block, first)
                second = jnp.where(far == s, block, second)
            total = None
            for beyond, index, weight in steps:
                value = jnp.where(beyond, take_lanes(second, index), take_lanes(first, index))
                total = weight * value if total is None else total + weight * value
            zmain[f * levels + l, own] = total
            picked = take_lanes(total, edge)
            at = f * levels + l
            if at == 0:
                zmain[both, own] = picked
            else:
                zmain[both, own] = jnp.where(group == at, picked, zmain[both, own])

    def pass_on(f):
        for d, source in enumerate(sources):
            across[f, d].wait_recv()
            relay[f, d] = remote(
                ring.at[source, f], ring.at[source, f], p_send.at[d, f], p_recv.at[d, f], la, partner
            )
            relay[f, d].start()

    zonal = []
    pass_on(0)
    for f in range(fields):
        if f + 1 < fields:
            pass_on(f + 1)
        beside[f].wait_recv()
        for d in range(halves - 1):
            relay[f, d].wait_recv()
        zonal_field(f)
        if f + 1 == fields:
            last = neighbours(zmain, zwest, zeast, both, 1, z_send, z_recv)
            for copy, goes, _ in last:
                guarded(goes, copy.start)
            zonal += last
        pair = pl.ds(8 + 2 * f, 2)
        rowset = straight(zmain, pl.ds(f * levels, levels), z_send.at[pair], z_recv.at[pair])
        for copy, goes, _ in rowset:
            guarded(goes, copy.start)
        zonal += rowset

    for copy, _, comes in params:
        guarded(comes, copy.wait_recv)
    tall = rows + HALO
    begin = HALO // 2
    body = pl.ds(begin, tall)
    wide = lax.broadcasted_iota(jnp.int32, (tall, width), 1)
    spot = wide & (2 * HALO - 1)
    line = lax.broadcasted_iota(jnp.int32, (tall, width), 0) + (la * rows - HALO // 2)
    inside = jnp.logical_and(line >= 0, line < bands * rows)

    def coefficients(cells, frac, coupling):
        inverse = jnp.where(inside, 1.0 / (1.0 + 4.0 * coupling), 0.0)
        linked = jnp.where(inside, coupling * inverse, 0.0)
        parts = [jnp.where(inside, part, 0.0) for part in merid_parts(cells, frac)]
        return parts, linked, inverse

    def joined(left, middle, right):
        return jnp.where(spot < HALO // 2, left, jnp.where(spot >= 3 * HALO // 2, right, middle))

    level_terms = [
        coefficients(pmain[l, body], pmain[2 + l, body], pmain[4 + l, body]) for l in range(levels)
    ]
    strip_terms = coefficients(
        *[joined(pwest[c, body], pmain[6 + c, body], peast[c, body]) for c in range(3)]
    )

    for copy, _, comes in zonal:
        guarded(comes, copy.wait_recv)

    def up_down(value):
        return pltpu.roll(value, 1, 0) + pltpu.roll(value, tall - 1, 0)

    parts, linked, inverse = strip_terms
    source = None
    for part, offset in zip(parts, range(-2, 4)):
        at = pl.ds(begin + offset, tall)
        term = part * joined(zwest[0, at], zmain[both, at], zeast[0, at])
        source = term if source is None else source + term
    scaled = source * inverse
    strips = [source]
    for sweep in range(SWEEPS - 1):
        last = strips[-1]
        around = up_down(last) + pltpu.roll(last, 1, 1) + pltpu.roll(last, width - 1, 1)
        strips.append(scaled + linked * around)

    first_lane, last_lane = wide == 0, wide == width - 1
    for at_field in range(both):
        parts, linked, inverse = level_terms[at_field % levels]
        source = None
        for part, offset in zip(parts, range(-2, 4)):
            term = part * zmain[at_field, pl.ds(begin + offset, tall)]
            source = term if source is None else source + term
        scaled = source * inverse
        ends = jnp.where(first_lane, HALO // 2 - 1, 3 * HALO // 2) + at_field * 2 * HALO
        phi = source
        for sweep in range(SWEEPS):
            beyond = take_lanes(strips[sweep], ends)
            before = jnp.where(first_lane, beyond, pltpu.roll(phi, 1, 1))
            after = jnp.where(last_lane, beyond, pltpu.roll(phi, width - 1, 1))
            phi = scaled + linked * (up_down(phi) + before + after)
        out[at_field // levels, at_field % levels] = phi[begin : begin + rows]

    for copy, goes, _ in params + zonal:
        guarded(goes, copy.wait_send)
    for f in range(fields):
        beside[f].wait_send()
        for d in range(halves - 1):
            across[f, d].wait_send()
            relay[f, d].wait_send()


def body(*args, bands, sectors):
    state = args[0]
    fields, levels, rows, width = state.shape
    both, halves = fields * levels, sectors // 2
    tall = rows + 2 * HALO
    f32 = jnp.float32
    spec = pl.BlockSpec(memory_space=pltpu.VMEM)
    pairs = pltpu.SemaphoreType.DMA((halves, fields))
    ten = pltpu.SemaphoreType.DMA((10,))
    many = pltpu.SemaphoreType.DMA((8 + 2 * fields,))
    hbm = pl.BlockSpec(memory_space=pltpu.HBM)
    small = (levels, rows, width)
    return pl.pallas_call(
        functools.partial(kernel, bands, sectors),
        out_shape=jax.ShapeDtypeStruct(state.shape, f32),
        in_specs=[hbm] * 7,
        out_specs=spec,
        scratch_shapes=[
            pltpu.VMEM((sectors,) + state.shape, f32),
            pltpu.VMEM((both + 1, tall, width), f32),
            pltpu.VMEM((1, tall, width), f32),
            pltpu.VMEM((1, tall, width), f32),
            pltpu.VMEM((9, tall, width), f32),
            pltpu.VMEM((3, tall, width), f32),
            pltpu.VMEM((3, tall, width), f32),
            pltpu.VMEM((levels, rows), jnp.int32),
            pltpu.VMEM(small, jnp.int32),
            pltpu.VMEM(small, f32),
            pltpu.VMEM(small, jnp.int32),
            pltpu.SemaphoreType.DMA((7,)),
            pairs, pairs, pairs, pairs, ten, ten, many, many,
        ],
        compiler_params=pltpu.CompilerParams(
            collective_id=0, has_side_effects=True, vmem_limit_bytes=63 * 2**20
        ),
    )(*args)


def solution(mesh):
    in_specs = (
        P(None, None, "lat", "lon"),
        P(None, "lat"),
        P(None, "lat", "lon"),
        P(None, "lat", "lon"),
        P(None, "lat", "lon"),
        P(None, "lat", "lon"),
        P(None, "lat", "lon"),
    )
    out_specs = P(None, None, "lat", "lon")
    run = functools.partial(body, bands=mesh.shape["lat"], sectors=mesh.shape["lon"])
    return jax.shard_map(run, mesh=mesh, in_specs=in_specs, out_specs=out_specs, check_vma=False)
```

profile of v0, /device:TPU:0, one launch (start us, length us, event | category | flops | bytes accessed | tf_op | source)
XLA Modules:
  0.0 17.2 jit_solution(18160122064503598595)
XLA Ops:
  0.0 15.6 %shard_map.73 = f32[4,2,24,128]{3,2,1,0:T(8,128)} custom-call(f32[4,2,24,128]{3,2,1,0:T(8,128)} %state.1, s32[2,24]{1,0:T(2,128)} %shift_in.1, s32[2,24,128]{2,1,0:T(8,128)} %zcells_in.1, f32[2,24,128]{2,1,0:T(8,128)} %zfrac_in.1, s32[2,24,128]{2,1,0:T(8,128)} %mcells_in.1, f32[2,24,128]{2,1,0:T(8,128)} %mfrac.1, f32[2,24,128]{2,1,0:T(8,128)} %coup.1), custom_call_target="tpu_custom_call" | custom-call | tf_op jit(solution)/shard_map/pallas_call | solution.py:341
  15.6 1.5 %copy.9 = f32[4,2,24,128]{3,2,1,0:T(8,128)} copy(f32[4,2,24,128]{3,2,1,0:T(8,128)} %shard_map.73) | data formatting | bytes 196608
where the time goes:
time: 17.3 us; the launch traced here: 17.2 us
  Pallas kernels  15.6 us (90%)
  local copies, waits for them, and re-layouts  1.54 us (9%)
    pallas_call x1, Pallas kernels, body(): pl.pallas_call(functools.partial(kernel, bands, sectors), out_shape=jax.S...  15.6 us
    unnamed x1, local copies, waits for them, and re-layouts  1.54 us

commit v1 on v0

--- a/solution.py
+++ b/solution.py
@@ -359,9 +359,9 @@
             pairs, pairs, pairs, pairs, ten, ten, many, many,
         ],
         compiler_params=pltpu.CompilerParams(
-            collective_id=0, has_side_effects=True, vmem_limit_bytes=63 * 2**20
+            collective_id=0, has_side_effects=True, vmem_limit_bytes=24 * 2**20
         ),
-    )(*args)
+    )(*[pltpu.with_memory_space_constraint(x, pltpu.HBM) for x in args])
 
 
 def solution(mesh):

time: 17.3 us -> 15.8 us (0.913)
  local copies, waits for them, and re-layouts: 1.54 us -> 0.64 us
  Pallas kernels: 15.6 us -> 15 us
    unnamed x1, local copies, waits for them, and re-layouts: 1.54 us -> 0.64 us
    pallas_call x1, Pallas kernels: 15.6 us -> 15 us  [body(): pl.pallas_call(functools.partial(kernel, bands, sectors), out_shape=jax.S...]
where the time goes in v1:
time: 15.8 us; the launch traced here: 15.6 us
  Pallas kernels  15 us (95%)
  local copies, waits for them, and re-layouts  0.64 us (4%)
    pallas_call x1, Pallas kernels, body(): pl.pallas_call(functools.partial(kernel, bands, sectors), out_shape=jax.S...  15 us
    unnamed x1, local copies, waits for them, and re-layouts  0.64 us

profile of v1, /device:TPU:0, one launch (start us, length us, event | category | flops | bytes accessed | tf_op | source)
XLA Modules:
  0.0 15.6 jit_solution(5227159101303258657)
XLA Ops:
  0.0 15.0 %shard_map.73 = f32[4,2,24,128]{3,2,1,0:T(8,128)S(1)} custom-call(f32[4,2,24,128]{3,2,1,0:T(8,128)} %state.1, s32[2,24]{1,0:T(2,128)} %shift_in.1, s32[2,24,128]{2,1,0:T(8,128)} %zcells_in.1, f32[2,24,128]{2,1,0:T(8,128)} %zfrac_in.1, s32[2,24,128]{2,1,0:T(8,128)} %mcells_in.1, f32[2,24,128]{2,1,0:T(8,128)} %mfrac.1, f32[2,24,128]{2,1,0:T(8,128)} %coup.1), custom_call_target="tpu_custom_call" | custom-call | tf_op jit(solution)/shard_map/pallas_call | solution.py:341
  15.0 0.6 %copy.9 = f32[4,2,24,128]{3,2,1,0:T(8,128)} copy(f32[4,2,24,128]{3,2,1,0:T(8,128)S(1)} %shard_map.73) | data formatting | bytes 196608

commit v2 on v1

--- a/solution.py
+++ b/solution.py
@@ -174,11 +174,12 @@
         pmain[l, own] = mcells[l].astype(jnp.float32)
     for at in range(3):
         low, high = pmain[2 * at, own], pmain[2 * at + 1, own]
-        packed = jnp.where((group & 1) == 0, take_lanes(low, edge), take_lanes(high, edge))
-        pmain[6 + at, own] = packed
+        picked = jnp.where((group & 1) == 0, take_lanes(low, edge), take_lanes(high, edge))
+        packed = picked if at == 0 else jnp.where((group // 2) == at, picked, packed)
+    pmain[6, own] = packed
 
     params = straight(pmain, pl.ds(0, 6), h_send.at[pl.ds(8, 2)], h_recv.at[pl.ds(8, 2)])
-    params += neighbours(pmain, pwest, peast, 6, 3, h_send, h_recv)
+    params += neighbours(pmain, pwest, peast, 6, 1, h_send, h_recv)
     for copy, goes, _ in params:
         guarded(goes, copy.start)
 
@@ -277,9 +278,9 @@
     level_terms = [
         coefficients(pmain[l, body], pmain[2 + l, body], pmain[4 + l, body]) for l in range(levels)
     ]
-    strip_terms = coefficients(
-        *[joined(pwest[c, body], pmain[6 + c, body], peast[c, body]) for c in range(3)]
-    )
+    edges = joined(pwest[0, body], pmain[6, body], peast[0, body])
+    pair = wide & (4 * HALO - 1)
+    strip_terms = coefficients(*[take_lanes(edges, pair + 4 * HALO * c) for c in range(3)])
 
     for copy, _, comes in zonal:
         guarded(comes, copy.wait_recv)
@@ -348,9 +349,9 @@
             pltpu.VMEM((both + 1, tall, width), f32),
             pltpu.VMEM((1, tall, width), f32),
             pltpu.VMEM((1, tall, width), f32),
-            pltpu.VMEM((9, tall, width), f32),
-            pltpu.VMEM((3, tall, width), f32),
-            pltpu.VMEM((3, tall, width), f32),
+            pltpu.VMEM((7, tall, width), f32),
+            pltpu.VMEM((1, tall, width), f32),
+            pltpu.VMEM((1, tall, width), f32),
             pltpu.VMEM((levels, rows), jnp.int32),
             pltpu.VMEM(small, jnp.int32),
             pltpu.VMEM(small, f32),

time: 15.8 us -> 15.6 us (0.987)
  Pallas kernels: 15 us -> 14.8 us
where the time goes in v2:
time: 15.6 us; the launch traced here: 15.5 us
  Pallas kernels  14.8 us (95%)
  local copies, waits for them, and re-layouts  0.64 us (4%)
    pallas_call x1, Pallas kernels, body(): pl.pallas_call(functools.partial(kernel, bands, sectors), out_shape=jax.S...  14.8 us
    unnamed x1, local copies, waits for them, and re-layouts  0.64 us

profile of v2, /device:TPU:0, one launch (start us, length us, event | category | flops | bytes accessed | tf_op | source)
XLA Modules:
  0.0 15.5 jit_solution(14439960387548321578)
XLA Ops:
  0.0 14.8 %shard_map.73 = f32[4,2,24,128]{3,2,1,0:T(8,128)S(1)} custom-call(f32[4,2,24,128]{3,2,1,0:T(8,128)} %state.1, s32[2,24]{1,0:T(2,128)} %shift_in.1, s32[2,24,128]{2,1,0:T(8,128)} %zcells_in.1, f32[2,24,128]{2,1,0:T(8,128)} %zfrac_in.1, s32[2,24,128]{2,1,0:T(8,128)} %mcells_in.1, f32[2,24,128]{2,1,0:T(8,128)} %mfrac.1, f32[2,24,128]{2,1,0:T(8,128)} %coup.1), custom_call_target="tpu_custom_call" | custom-call | tf_op jit(solution)/shard_map/pallas_call | solution.py:342
  14.8 0.6 %copy.9 = f32[4,2,24,128]{3,2,1,0:T(8,128)} copy(f32[4,2,24,128]{3,2,1,0:T(8,128)S(1)} %shard_map.73) | data formatting | bytes 196608

commit v3 on v2

--- a/solution.py
+++ b/solution.py
@@ -249,7 +249,6 @@
             last = neighbours(zmain, zwest, zeast, both, 1, z_send, z_recv)
             for copy, goes, _ in last:
                 guarded(goes, copy.start)
-            zonal += last
         pair = pl.ds(8 + 2 * f, 2)
         rowset = straight(zmain, pl.ds(f * levels, levels), z_send.at[pair], z_recv.at[pair])
         for copy, goes, _ in rowset:
@@ -284,6 +283,16 @@
 
     for copy, _, comes in zonal:
         guarded(comes, copy.wait_recv)
+    origins = []
+    for at_field in range(both):
+        source = None
+        for part, offset in zip(level_terms[at_field % levels][0], range(-2, 4)):
+            term = part * zmain[at_field, pl.ds(begin + offset, tall)]
+            source = term if source is None else source + term
+        origins.append(source)
+
+    for copy, _, comes in last:
+        guarded(comes, copy.wait_recv)
 
     def up_down(value):
         return pltpu.roll(value, 1, 0) + pltpu.roll(value, tall - 1, 0)
@@ -297,17 +306,14 @@
     scaled = source * inverse
     strips = [source]
     for sweep in range(SWEEPS - 1):
-        last = strips[-1]
-        around = up_down(last) + pltpu.roll(last, 1, 1) + pltpu.roll(last, width - 1, 1)
+        phi = strips[-1]
+        around = up_down(phi) + pltpu.roll(phi, 1, 1) + pltpu.roll(phi, width - 1, 1)
         strips.append(scaled + linked * around)
 
     first_lane, last_lane = wide == 0, wide == width - 1
     for at_field in range(both):
-        parts, linked, inverse = level_terms[at_field % levels]
-        source = None
-        for part, offset in zip(parts, range(-2, 4)):
-            term = part * zmain[at_field, pl.ds(begin + offset, tall)]
-            source = term if source is None else source + term
+        _, linked, inverse = level_terms[at_field % levels]
+        source = origins[at_field]
         scaled = source * inverse
         ends = jnp.where(first_lane, HALO // 2 - 1, 3 * HALO // 2) + at_field * 2 * HALO
         phi = source
@@ -318,7 +324,7 @@
             phi = scaled + linked * (up_down(phi) + before + after)
         out[at_field // levels, at_field % levels] = phi[begin : begin + rows]
 
-    for copy, goes, _ in params + zonal:
+    for copy, goes, _ in params + zonal + last:
         guarded(goes, copy.wait_send)
     for f in range(fields):
         beside[f].wait_send()

time: 15.6 us -> 15.7 us (level)
  no operation moved by 1% of the time
where the time goes in v3:
time: 15.7 us; the launch traced here: 15.6 us
  Pallas kernels  14.9 us (95%)
  local copies, waits for them, and re-layouts  0.64 us (4%)
    pallas_call x1, Pallas kernels, body(): pl.pallas_call(functools.partial(kernel, bands, sectors), out_shape=jax.S...  14.9 us
    unnamed x1, local copies, waits for them, and re-layouts  0.64 us

profile of v3, /device:TPU:0, one launch (start us, length us, event | category | flops | bytes accessed | tf_op | source)
XLA Modules:
  0.0 15.6 jit_solution(8992248861140175960)
XLA Ops:
  0.0 14.9 %shard_map.73 = f32[4,2,24,128]{3,2,1,0:T(8,128)S(1)} custom-call(f32[4,2,24,128]{3,2,1,0:T(8,128)} %state.1, s32[2,24]{1,0:T(2,128)} %shift_in.1, s32[2,24,128]{2,1,0:T(8,128)} %zcells_in.1, f32[2,24,128]{2,1,0:T(8,128)} %zfrac_in.1, s32[2,24,128]{2,1,0:T(8,128)} %mcells_in.1, f32[2,24,128]{2,1,0:T(8,128)} %mfrac.1, f32[2,24,128]{2,1,0:T(8,128)} %coup.1), custom_call_target="tpu_custom_call" | custom-call | tf_op jit(solution)/shard_map/pallas_call | solution.py:348
  14.9 0.6 %copy.9 = f32[4,2,24,128]{3,2,1,0:T(8,128)} copy(f32[4,2,24,128]{3,2,1,0:T(8,128)S(1)} %shard_map.73) | data formatting | bytes 196608

commit v4 on v2

--- a/solution.py
+++ b/solution.py
@@ -180,8 +180,6 @@
 
     params = straight(pmain, pl.ds(0, 6), h_send.at[pl.ds(8, 2)], h_recv.at[pl.ds(8, 2)])
     params += neighbours(pmain, pwest, peast, 6, 1, h_send, h_recv)
-    for copy, goes, _ in params:
-        guarded(goes, copy.start)
 
     for load in loads[4:]:
         load.wait()
@@ -241,6 +239,9 @@
     for f in range(fields):
         if f + 1 < fields:
             pass_on(f + 1)
+        if f + 2 == fields:
+            for copy, goes, _ in params:
+                guarded(goes, copy.start)
         beside[f].wait_recv()
         for d in range(halves - 1):
             relay[f, d].wait_recv()

time: 15.6 us -> 15.7 us (level); the launches traced: 15.5 us -> 15.4 us
  no operation moved by 1% of the time
where the time goes in v4:
time: 15.7 us; the launch traced here: 15.4 us
  Pallas kernels  14.7 us (94%)
  local copies, waits for them, and re-layouts  0.64 us (4%)
    pallas_call x1, Pallas kernels, body(): pl.pallas_call(functools.partial(kernel, bands, sectors), out_shape=jax.S...  14.7 us
    unnamed x1, local copies, waits for them, and re-layouts  0.64 us

profile of v4, /device:TPU:0, one launch (start us, length us, event | category | flops | bytes accessed | tf_op | source)
XLA Modules:
  0.0 15.4 jit_solution(278230629734033552)
XLA Ops:
  0.0 14.7 %shard_map.73 = f32[4,2,24,128]{3,2,1,0:T(8,128)S(1)} custom-call(f32[4,2,24,128]{3,2,1,0:T(8,128)} %state.1, s32[2,24]{1,0:T(2,128)} %shift_in.1, s32[2,24,128]{2,1,0:T(8,128)} %zcells_in.1, f32[2,24,128]{2,1,0:T(8,128)} %zfrac_in.1, s32[2,24,128]{2,1,0:T(8,128)} %mcells_in.1, f32[2,24,128]{2,1,0:T(8,128)} %mfrac.1, f32[2,24,128]{2,1,0:T(8,128)} %coup.1), custom_call_target="tpu_custom_call" | custom-call | tf_op jit(solution)/shard_map/pallas_call | solution.py:343
  14.8 0.6 %copy.9 = f32[4,2,24,128]{3,2,1,0:T(8,128)} copy(f32[4,2,24,128]{3,2,1,0:T(8,128)S(1)} %shard_map.73) | data formatting | bytes 196608
